TPU v7x, 32 devices: a whole 2x2x4 slice. The times are simulated.
32 devices in a mesh: tile: 4 (over z), dir: 8 (over y, x, core).
Axes of the slice: x: 2, y: 2, z: 4, core: 2. Of those that a mesh axis runs over, the one named last changes fastest.
Arguments:
- spectrum: float32 [48, 36, 8192], P('dir', None, 'tile'), may hold values from 0.2 to 5
- active_points: int32 [4], P('tile'), may hold values from 1024 to 2048, as said below
- send_list: int32 [4, 4, 128], P('tile'), may hold values from 0 to 2047, as said below
- neighbor: int32 [4, 8192], P(None, 'tile'), may hold values from 0 to 2559, as said below
- depth_class: int32 [8192], P('tile'), may hold values from 0 to 3
- group_speed: float32 [4, 36], replicated, may hold values from 0.05 to 0.35
- refraction: float32 [8192], P('tile'), may hold values from -0.45 to 0.45
- kernel: float32 [1728, 1728], P('dir'), may hold values from -0.078125 to 0.078125
- wave_weight: float32 [36], replicated, may hold values from 5e-05 to 0.0005
Outputs:
- new_spectrum: float32 [48, 36, 8192], P('dir', None, 'tile')
Inputs may be any that keep to these rules, and one draw needn't show every extreme that they name: `active_points`: at least one tile has all 2048 points in use. send_list[s, t, j] is a point number within tile s. `neighbor`: a value v below 2048 names point v of the same tile; v = 2048 + s * 128 + j names the point send_list[s, t, j] of tile s.
All inputs are finite; a program needn't handle non-finite values.
Results may differ from a plain program's by a relative error of at most 0.0001.
Values sent between devices are 32-bit elements; how exact they have to be, the bound alone decides.
A program may use at most 128 MiB of HBM per device.

v0:
```python
import math

import jax
import jax.numpy as jnp
from jax import lax
from jax.sharding import PartitionSpec as P

SUB = 5


def extended_2(value, sides, width):
    for axis, dim in sides:
        devices, length = (lax.axis_size(axis), value.shape[dim])
        up = [(i, (i + 1) % devices) for i in range(devices)]
        down = [(j, i) for i, j in up]
        last = lax.slice_in_dim(value, length - width, length, axis=dim)
        first = lax.slice_in_dim(value, 0, width, axis=dim)
        before = lax.ppermute(last, axis, up)
        after = lax.ppermute(first, axis, down)
        value = jnp.concatenate([before, value, after], axis=dim)
    return value


def source_substep(state, kernel, wave_weight):
    dirs_local, freqs, points = state.shape
    piece = lax.all_gather(state, "dir", axis=0, tiled=True)
    count = piece.shape[0] * freqs
    block = piece.reshape(count, points)
    product = jnp.dot(
        kernel, block, precision=lax.Precision.HIGHEST, preferred_element_type=jnp.float32
    )
    steep = jnp.sum(wave_weight[None, :, None] * piece * piece, axis=(0, 1))
    product, steep = (product, steep)
    return (state + product.reshape(dirs_local, freqs, points)) / (1.0 + steep)[None, None, :]


def turn_shards(moved, refraction):
    padded = extended_2(moved, (("dir", 0),), 1)
    lower = padded[:-2]
    upper = padded[2:]
    forward = jnp.maximum(refraction, 0.0)[None, None, :]
    backward = jnp.maximum(-refraction, 0.0)[None, None, :]
    return moved + forward * (lower - moved) + backward * (upper - moved)


def per_device(
    spectrum,
    active_points,
    send_list,
    neighbor,
    depth_class,
    group_speed,
    refraction,
    kernel,
    wave_weight,
):
    dirs_local, freqs, points = spectrum.shape
    tiles = lax.axis_size("tile")
    groups = lax.axis_size("dir")
    faces = send_list.shape[2]
    mask = (jnp.arange(points, dtype=jnp.int32) < active_points[0]).astype(jnp.float32)
    field = spectrum * mask[None, None, :]
    outgoing = jnp.take(field, send_list[0], axis=2)
    incoming = lax.all_to_all(outgoing, "tile", split_axis=2, concat_axis=2, tiled=True)
    extended = jnp.concatenate([field, incoming.reshape(dirs_local, freqs, tiles * faces)], axis=2)
    total_dirs = dirs_local * groups
    first_dir = lax.axis_index("dir") * dirs_local
    theta = (first_dir + jnp.arange(dirs_local, dtype=jnp.int32)).astype(jnp.float32) * (
        2.0 * math.pi / total_dirs
    )
    angles = jnp.arange(4).astype(jnp.float32) * (math.pi / 2.0)
    upwind = jnp.maximum(jnp.cos(theta[:, None] - angles[None, :]), 0.0)
    onehot = (
        depth_class[None, :] == jnp.arange(group_speed.shape[0], dtype=jnp.int32)[:, None]
    ).astype(jnp.float32)
    courant = jnp.sum(group_speed[:, :, None] * onehot[:, None, :], axis=0)
    flow = jnp.zeros_like(field)
    for which in range(4):
        flow = flow + upwind[:, which][:, None, None] * (
            jnp.take(extended, neighbor[which], axis=2) - field
        )
    moved = field + courant[None, :, :] * flow
    state = turn_shards(moved, refraction)
    for step in range(SUB):
        state = source_substep(state, kernel, wave_weight)
    return state * mask[None, None, :]


def solution(mesh):
    return jax.shard_map(
        per_device,
        mesh=mesh,
        in_specs=(
            P("dir", None, "tile"),
            P("tile"),
            P("tile", None, None),
            P(None, "tile"),
            P("tile"),
            P(),
            P("tile"),
            P("dir", None),
            P(),
        ),
        out_specs=P("dir", None, "tile"),
        check_vma=False,
    )
```

profile of v0, /device:TPU:1, one launch (start us, length us, event | category | flops | bytes accessed | tf_op | source)
XLA Modules:
  0.0 831.4 jit_solution(12670232778511380259)
XLA Ops:
  15.2 5.8 gather_fusion
  38.1 6.5 all-to-all-done
  51.3 7.2 copy.100
  58.5 19.7 %gather_fusion.4 = f32[2048,6,36]{2,1,0:T(8,128)} fusion(f32[6,36,2560]{1,0,2:T(8,128)} %copy.100, s32[2048]{0:T(1024)S(1)} %copy-done.9), kind=kCustom, calls=%fused_computation.3.clone | custom fusion | bytes 3547136 | tf_op jit(solution)/shard_map/jit(_take)/gather | solution.py:80
  78.2 6.0 copy.107
  84.2 19.7 %gather_fusion.3 = f32[2048,6,36]{2,1,0:T(8,128)} fusion(f32[6,36,2560]{1,0,2:T(8,128)} %copy.100, s32[2048]{0:T(1024)S(1)} %copy-done.8), kind=kCustom, calls=%fused_computation.2.clone | custom fusion | bytes 3547136 | tf_op jit(solution)/shard_map/jit(_take)/gather | solution.py:80
  104.0 6.1 copy.105
  110.1 19.7 %gather_fusion.2 = f32[2048,6,36]{2,1,0:T(8,128)} fusion(f32[6,36,2560]{1,0,2:T(8,128)} %copy.100, s32[2048]{0:T(1024)S(1)} %copy-done.7), kind=kCustom, calls=%fused_computation.1.clone | custom fusion | bytes 3547136 | tf_op jit(solution)/shard_map/jit(_take)/gather | solution.py:80
  129.8 6.0 copy.103
  135.8 19.7 %gather_fusion.1 = f32[2048,6,36]{2,1,0:T(8,128)} fusion(f32[6,36,2560]{1,0,2:T(8,128)} %copy.100, s32[2048]{0:T(1024)S(1)} %fusion.22), kind=kCustom, calls=%fused_computation.clone | custom fusion | bytes 3547136 | tf_op jit(solution)/shard_map/jit(_take)/gather | solution.py:80
  155.6 6.0 copy.101
  170.3 6.1 collective-permute-done.1
  179.8 84.4 %all-gather.6.cloned.1.call-done = f32[48,36,2048]{2,1,0:T(8,128)} async-done(((f32[6,36,2048]{2,1,0:T(8,128)}), f32[48,36,2048]{2,1,0:T(8,128)}) %all-gather.6.cloned.1.call-update) | async-done | bytes 14155792 | tf_op jit(solution)/shard_map/all_gather | solution.py:26
  264.2 7.3 fusion
  271.5 14.7 %reshape.131 = f32[1728,2048]{1,0:T(8,128)} reshape(f32[48,36,2048]{2,1,0:T(8,128)} %all-gather.6.cloned.1.call-done) | data formatting | bytes 28311552 | tf_op jit(solution)/shard_map/reshape | solution.py:28
  286.2 15.4 %convolution_bitcast_fusion.4 = f32[216,2048]{1,0:T(8,128)} fusion(f32[1728,2048]{1,0:T(8,128)} %reshape.131, f32[216,1728]{1,0:T(8,128)S(1)} %copy-done), kind=kOutput, calls=%fused_computation.19 | convolution fusion | flops 9172942848 | bytes 17418240 | tf_op jit(solution)/shard_map/dot_general | solution.py:29
  308.2 85.3 %all-gather.8.cloned.1.call-done = f32[48,36,2048]{2,1,0:T(8,128)} async-done(((f32[6,36,2048]{2,1,0:T(8,128)}), f32[48,36,2048]{2,1,0:T(8,128)}) %all-gather.8.cloned.1.call-update) | async-done | bytes 14155792 | tf_op jit(solution)/shard_map/all_gather | solution.py:26
  393.5 14.7 %reshape.133 = f32[1728,2048]{1,0:T(8,128)} reshape(f32[48,36,2048]{2,1,0:T(8,128)} %all-gather.8.cloned.1.call-done) | data formatting | bytes 28311552 | tf_op jit(solution)/shard_map/reshape | solution.py:28
  408.2 15.4 %convolution_bitcast_fusion.3 = f32[216,2048]{1,0:T(8,128)} fusion(f32[1728,2048]{1,0:T(8,128)} %reshape.133, f32[216,1728]{1,0:T(8,128)S(1)} %copy-done), kind=kOutput, calls=%fused_computation.18 | convolution fusion | flops 9172942848 | bytes 17418240 | tf_op jit(solution)/shard_map/dot_general | solution.py:29
  423.6 7.3 fusion.1
  437.6 85.1 %all-gather.10.cloned.1.call-done = f32[48,36,2048]{2,1,0:T(8,128)} async-done(((f32[6,36,2048]{2,1,0:T(8,128)}), f32[48,36,2048]{2,1,0:T(8,128)}) %all-gather.10.cloned.1.call-update) | async-done | bytes 14155792 | tf_op jit(solution)/shard_map/all_gather | solution.py:26
  522.6 14.7 %reshape.135 = f32[1728,2048]{1,0:T(8,128)} reshape(f32[48,36,2048]{2,1,0:T(8,128)} %all-gather.10.cloned.1.call-done) | data formatting | bytes 28311552 | tf_op jit(solution)/shard_map/reshape | solution.py:28
  537.3 15.4 %convolution_bitcast_fusion.2 = f32[216,2048]{1,0:T(8,128)} fusion(f32[1728,2048]{1,0:T(8,128)} %reshape.135, f32[216,1728]{1,0:T(8,128)S(1)} %copy-done), kind=kOutput, calls=%fused_computation.17 | convolution fusion | flops 9172942848 | bytes 17418240 | tf_op jit(solution)/shard_map/dot_general | solution.py:29
  552.7 7.3 fusion.2
  566.4 85.4 %all-gather.12.cloned.1.call-done = f32[48,36,2048]{2,1,0:T(8,128)} async-done(((f32[6,36,2048]{2,1,0:T(8,128)}), f32[48,36,2048]{2,1,0:T(8,128)}) %all-gather.12.cloned.1.call-update) | async-done | bytes 14155792 | tf_op jit(solution)/shard_map/all_gather | solution.py:26
  651.8 14.7 %reshape.137 = f32[1728,2048]{1,0:T(8,128)} reshape(f32[48,36,2048]{2,1,0:T(8,128)} %all-gather.12.cloned.1.call-done) | data formatting | bytes 28311552 | tf_op jit(solution)/shard_map/reshape | solution.py:28
  666.5 15.4 %convolution_bitcast_fusion.1 = f32[216,2048]{1,0:T(8,128)} fusion(f32[1728,2048]{1,0:T(8,128)} %reshape.137, f32[216,1728]{1,0:T(8,128)S(1)} %copy-done), kind=kOutput, calls=%fused_computation.16 | convolution fusion | flops 9172942848 | bytes 17418240 | tf_op jit(solution)/shard_map/dot_general | solution.py:29
  681.9 7.3 fusion.3
  695.3 85.6 %all-gather.14.cloned.1.call-done = f32[48,36,2048]{2,1,0:T(8,128)} async-done(((f32[6,36,2048]{2,1,0:T(8,128)}), f32[48,36,2048]{2,1,0:T(8,128)}) %all-gather.14.cloned.1.call-update) | async-done | bytes 14155792 | tf_op jit(solution)/shard_map/all_gather | solution.py:26
  780.9 14.7 %reshape.139 = f32[1728,2048]{1,0:T(8,128)} reshape(f32[48,36,2048]{2,1,0:T(8,128)} %all-gather.14.cloned.1.call-done) | data formatting | bytes 28311552 | tf_op jit(solution)/shard_map/reshape | solution.py:28
  795.6 15.6 %convolution_bitcast_fusion = f32[216,2048]{1,0:T(8,128)} fusion(f32[1728,2048]{1,0:T(8,128)} %reshape.139, f32[216,1728]{1,0:T(8,128)S(1)} %copy-done), kind=kOutput, calls=%fused_computation.15 | convolution fusion | flops 9172942848 | bytes 17418240 | tf_op jit(solution)/shard_map/dot_general | solution.py:29
  811.2 7.3 fusion.4
  (98 shorter events, 75.8 us)
Async XLA Ops:
  6.5 279.7 %copy-start = (f32[216,1728]{1,0:T(8,128)S(1)}, f32[216,1728]{1,0:T(8,128)}, u32[]{:S(2)}) copy-start(f32[216,1728]{1,0:T(8,128)} %param.18) | copy-start | bytes 4478980
  21.0 11.3 %copy-start.17 = (f32[4,36]{1,0:T(4,128)S(1)}, f32[4,36]{1,0:T(4,128)}, u32[]{:S(2)}) copy-start(f32[4,36]{1,0:T(4,128)} %param.16) | copy-start | bytes 1732
  21.0 11.4 %copy-start.11 = (s32[2048]{0:T(1024)S(1)}, s32[2048]{0:T(1024)}, u32[]{:S(2)}) copy-start(s32[2048]{0:T(1024)} %param.15) | copy-start | bytes 24580
  25.7 18.8 %all-to-all-start = ((f32[6,36,4,128]{3,1,0,2:T(8,128)}), f32[6,36,4,128]{3,1,0,2:T(8,128)}, u32[]{:S(2)}, u32[]{:S(2)}) async-start(f32[6,36,4,128]{3,1,0,2:T(8,128)} %select_bitcast_fusion), calls=%async_computation | async-start | bytes 983040 | tf_op jit(solution)/shard_map/all_to_all | solution.py:64
  31.2 233.1 %all-gather.6.cloned.1.call-start = ((), (), s32[]{:S(2)}) async-start(), calls=%async_computation.1 | async-start | bytes 17694720 | tf_op jit(solution)/shard_map/all_gather | solution.py:26
  51.3 7.2 copy-start.9
  78.2 6.0 copy-start.8
  104.0 6.1 copy-start.7
  155.6 6.1 copy-start.13
  155.6 6.1 copy-start.14
  155.6 6.1 copy-start.15
  155.6 6.1 copy-start.16
  167.0 3.4 copy-start.12
  167.4 9.0 %collective-permute-start.1 = (f32[1,36,2048]{2,0,1:T(1,128)S(1)}, f32[1,36,2048]{2,0,1:T(1,128)S(1)}, u32[]{:S(2)}, u32[]{:S(2)}) collective-permute-start(f32[1,36,2048]{2,0,1:T(1,128)S(1)} %copy.110), channel_id=1, source_target_pairs={{1,0},{2,1},{3,2},{4,3},{5,4},{6,5},{7,6},{0,7},{9,8},{10,9},{11,1... | collective-permute-start | bytes 884744 | tf_op jit(solution)/shard_map/ppermute | solution.py:19
  169.2 7.9 collective-permute-start
  176.5 0.7 copy-start.5
  177.1 0.7 copy-start.6
  179.5 84.7 %copy-start.10 = (f32[36]{0:T(128)S(1)}, f32[36]{0:T(128)}, u32[]{:S(2)}) copy-start(f32[36]{0:T(128)} %param.19) | copy-start | bytes 436
  179.5 214.0 %all-gather.8.cloned.1.call-start = ((), (), s32[]{:S(2)}) async-start(), calls=%async_computation.2 | async-start | bytes 17694720 | tf_op jit(solution)/shard_map/all_gather | solution.py:26
  307.9 214.7 %all-gather.10.cloned.1.call-start = ((), (), s32[]{:S(2)}) async-start(), calls=%async_computation.3 | async-start | bytes 17694720 | tf_op jit(solution)/shard_map/all_gather | solution.py:26
  430.8 2.9 copy-start.1
  437.1 214.7 %all-gather.12.cloned.1.call-start = ((), (), s32[]{:S(2)}) async-start(), calls=%async_computation.4 | async-start | bytes 17694720 | tf_op jit(solution)/shard_map/all_gather | solution.py:26
  560.0 2.9 copy-start.2
  566.2 214.7 %all-gather.14.cloned.1.call-start = ((), (), s32[]{:S(2)}) async-start(), calls=%async_computation.5 | async-start | bytes 17694720 | tf_op jit(solution)/shard_map/all_gather | solution.py:26
  689.1 2.9 copy-start.3
  818.5 2.9 copy-start.4
Sparse Core Ops, SparseCore 0:
  179.6 84.5 all-gather.5
  308.0 85.4 all-gather.7
  437.2 85.4 all-gather.9
  566.3 85.4 all-gather.11
  695.5 85.4 all-gather.13
where the time goes:
time: 842 us; the launch traced here: 831 us
  waiting for transfers between devices  439 us (52%)
  local copies, waits for them, and re-layouts  219 us (26%)
  matrix products  77 us (9%)
  other arithmetic  73.4 us (9%)
  between operations  14.2 us (2%)
  starting transfers between devices  9.36 us (1%)
    all_gather x5, waiting for transfers between devices, source_substep(): piece = lax.all_gather(state, 'dir', axis=0, tiled=True)  426 us
    gather x8, local copies, waits for them, and re-layouts, per_device(): jnp.take(extended, neighbor[which], axis=2) - field  103 us
    dot_general x5, matrix products, source_substep(): jnp.dot(kernel, block, precision=lax.Precision.HIGHEST, preferred_element...  77 us
    reshape x5, local copies, waits for them, and re-layouts, source_substep(): block = piece.reshape(count, points)  73.5 us
    reduce_sum x5, other arithmetic, source_substep(): steep = jnp.sum(wave_weight[None, :, None] * piece * piece, axis=(0, 1))  36.4 us
  transfers between devices with their start and end apart: 8, of which 8 were waited for; matrix products, arithmetic and copies ran while one was open for 1% of the time, Pallas kernels for 0%

commit v1 on v0

v1 whole, which is shorter than its diff:
```python
import functools
import math

import jax
import jax.numpy as jnp
from jax import lax
from jax.experimental import pallas as pl
from jax.experimental.pallas import tpu as pltpu
from jax.sharding import PartitionSpec as P

SUB = 5
F32 = jnp.float32
BF16 = jnp.bfloat16


def split2(x):
    hi = x.astype(BF16)
    return hi, (x - hi.astype(F32)).astype(BF16)


def pick_kernel(ext_ref, send_ref, out_ref):
    points = ext_ref.shape[1]
    want = lax.broadcasted_iota(jnp.int32, (points, send_ref.shape[1]), 0)
    pick = jnp.where(want == send_ref[...], 1.0, 0.0).astype(BF16)
    total = None
    rest = ext_ref[...]
    for _ in range(3):
        part = rest.astype(BF16)
        rest = rest - part.astype(F32)
        got = jnp.dot(part, pick, preferred_element_type=F32)
        total = got if total is None else total + got
    out_ref[...] = total


def move_kernel(ways, field_ref, halo_ref, idx_ref, up_ref, depth_ref, speed_ref, block_ref, out_ref, parts_ref):
    rows, points = field_ref.shape
    width = points + halo_ref.shape[1]

    @pl.when(pl.program_id(0) == 0)
    def _():
        for ref, lo in ((field_ref, 0), (halo_ref, points)):
            hi_part, lo_part = split2(ref[...])
            parts_ref[0, :, lo:lo + ref.shape[1]] = hi_part
            parts_ref[1, :, lo:lo + ref.shape[1]] = lo_part

    own = block_ref[...]
    cols = own.shape[1]
    number = lax.broadcasted_iota(jnp.int32, (width, cols), 0)
    flow = None
    for k in range(ways):
        pick = jnp.where(number == idx_ref[k:k + 1, :], 1.0, 0.0).astype(BF16)
        got = jnp.dot(parts_ref[0], pick, preferred_element_type=F32)
        got = got + jnp.dot(parts_ref[1], pick, preferred_element_type=F32)
        term = up_ref[:, k:k + 1] * (got - own)
        flow = term if flow is None else flow + term
    courant = None
    for c in range(speed_ref.shape[1]):
        term = speed_ref[:, c:c + 1] * jnp.where(depth_ref[...] == c, 1.0, 0.0)
        courant = term if courant is None else courant + term
    out_ref[0] = own + courant * flow


def source_kernel(freqs, blocks, moved_ref, turn_ref, mask_ref, weight_ref, kernel_ref, out_ref, khi_ref, klo_ref, shi_ref, slo_ref):
    count, points = out_ref.shape
    size = count // blocks

    @pl.loop(0, blocks)
    def _(i):
        rows = pl.ds(pl.multiple_of(i * size, size), size)
        hi, lo = split2(kernel_ref[rows, :])
        khi_ref[rows, :] = hi
        klo_ref[rows, :] = lo

    moved = moved_ref[...]
    forward = jnp.maximum(turn_ref[...], 0.0)
    backward = jnp.maximum(-turn_ref[...], 0.0)
    lower = pltpu.roll(moved, freqs, 0)
    upper = pltpu.roll(moved, count - freqs, 0)
    out_ref[...] = moved + forward * (lower - moved) + backward * (upper - moved)
    for step in range(SUB):
        state = out_ref[...]
        steep = jnp.sum(weight_ref[...] * (state * state), axis=0, keepdims=True)
        scale = 1.0 / (1.0 + steep)
        if step == SUB - 1:
            scale = scale * mask_ref[...]
        hi, lo = split2(state)
        shi_ref[...] = hi
        slo_ref[...] = lo

        @pl.loop(0, blocks)
        def _(i):
            rows = pl.ds(pl.multiple_of(i * size, size), size)
            khi = khi_ref[rows, :]
            product = jnp.dot(khi, shi_ref[...], preferred_element_type=F32)
            product = product + jnp.dot(khi, slo_ref[...], preferred_element_type=F32)
            product = product + jnp.dot(klo_ref[rows, :], shi_ref[...], preferred_element_type=F32)
            out_ref[rows, :] = (out_ref[rows, :] + product) * scale


def per_device(
    spectrum,
    active_points,
    send_list,
    neighbor,
    depth_class,
    group_speed,
    refraction,
    kernel,
    wave_weight,
):
    dirs_local, freqs, points = spectrum.shape
    tiles = lax.axis_size("tile")
    groups = lax.axis_size("dir")
    faces = send_list.shape[2]
    classes = group_speed.shape[0]
    rows = dirs_local * freqs
    count = rows * groups
    cols = points // groups
    total_dirs = dirs_local * groups
    group = lax.axis_index("dir")
    vmem = pltpu.CompilerParams(vmem_limit_bytes=56 * 2**20)
    whole = functools.partial(pl.BlockSpec, memory_space=pltpu.VMEM)

    full = lax.all_gather(kernel, "dir", axis=0, tiled=True)

    mask = (jnp.arange(points, dtype=jnp.int32) < active_points[0]).astype(F32)
    field = spectrum.reshape(rows, points) * mask[None, :]
    send = send_list.reshape(1, tiles * faces)
    outgoing = pl.pallas_call(
        pick_kernel,
        out_shape=jax.ShapeDtypeStruct((rows, tiles * faces), F32),
        in_specs=[whole(), whole()],
        out_specs=whole(),
        compiler_params=vmem,
        name="pick",
    )(field, send)
    incoming = lax.all_to_all(outgoing, "tile", split_axis=1, concat_axis=1, tiled=True)

    first_dir = group * dirs_local
    theta = (first_dir + jnp.arange(dirs_local, dtype=jnp.int32)).astype(F32) * (2.0 * math.pi / total_dirs)
    angles = jnp.arange(4).astype(F32) * (math.pi / 2.0)
    upwind = jnp.maximum(jnp.cos(theta[:, None] - angles[None, :]), 0.0)
    links = neighbor
    ways = 4
    quarter = total_dirs // 4
    if total_dirs % 4 == 0 and quarter % dirs_local == 0:
        k0 = first_dir // quarter
        pair = jnp.stack([k0, (k0 + 1) % 4])
        upwind = jnp.take(upwind, pair, axis=1)
        links = jnp.take(neighbor, pair, axis=0)
        ways = 2
    up_rows = jnp.repeat(upwind, freqs, axis=0)
    speed_rows = jnp.tile(group_speed.T, (dirs_local, 1))

    moved = pl.pallas_call(
        functools.partial(move_kernel, ways),
        grid=(groups,),
        out_shape=jax.ShapeDtypeStruct((groups, rows, cols), F32),
        in_specs=[
            whole(),
            whole(),
            pl.BlockSpec((ways, cols), lambda i: (0, i)),
            whole(),
            pl.BlockSpec((1, cols), lambda i: (0, i)),
            whole(),
            pl.BlockSpec((rows, cols), lambda i: (0, i)),
        ],
        out_specs=pl.BlockSpec((1, rows, cols), lambda i: (i, 0, 0)),
        scratch_shapes=[pltpu.VMEM((2, rows, points + tiles * faces), BF16)],
        compiler_params=vmem,
        name="move",
    )(field, incoming, links, up_rows, depth_class[None, :], speed_rows, field)

    mine = lax.all_to_all(moved, "dir", split_axis=0, concat_axis=0, tiled=True)
    start = group * cols
    turn = lax.dynamic_slice_in_dim(refraction, start, cols)[None, :]
    my_mask = lax.dynamic_slice_in_dim(mask, start, cols)[None, :]
    weights = jnp.tile(wave_weight, total_dirs)[:, None]
    blocks = 2
    state = pl.pallas_call(
        functools.partial(source_kernel, freqs, blocks),
        out_shape=jax.ShapeDtypeStruct((count, cols), F32),
        in_specs=[whole()] * 5,
        out_specs=whole(),
        scratch_shapes=[
            pltpu.VMEM((count, count), BF16),
            pltpu.VMEM((count, count), BF16),
            pltpu.VMEM((count, cols), BF16),
            pltpu.VMEM((count, cols), BF16),
        ],
        compiler_params=vmem,
        name="source",
    )(mine.reshape(count, cols), turn, my_mask, weights, full)
    back = lax.all_to_all(state.reshape(groups, rows, cols), "dir", split_axis=0, concat_axis=0, tiled=True)
    return jnp.transpose(back, (1, 0, 2)).reshape(dirs_local, freqs, points)


def solution(mesh):
    return jax.shard_map(
        per_device,
        mesh=mesh,
        in_specs=(
            P("dir", None, "tile"),
            P("tile"),
            P("tile", None, None),
            P(None, "tile"),
            P("tile"),
            P(),
            P("tile"),
            P("dir", None),
            P(),
        ),
        out_specs=P("dir", None, "tile"),
        check_vma=False,
    )
```

time: 842 us -> 175 us (0.21); the launches traced: 831 us -> 174 us
  waiting for transfers between devices: 439 us -> 51.4 us
  local copies, waits for them, and re-layouts: 219 us -> 12.5 us
  matrix products: 77 us -> 0 us
  other arithmetic: 73.4 us -> 2.42 us
  Pallas kernels: 0 us -> 56.7 us
  blocking collectives: 0 us -> 25.9 us
    all_gather x5 -> x1, waiting for transfers between devices: 426 us -> 6.97 us  [per_device(): full = lax.all_gather(kernel, 'dir', axis=0, tiled=True)]
    gather x10 -> x2, local copies, waits for them, and re-layouts: 112 us -> 1.13 us  [the longest x1 0.57 us: per_device(): links = jnp.take(neighbor, pair, axis=0)]
    reshape x11 -> x4, local copies, waits for them, and re-layouts: 89.5 us -> 3.99 us  [the longest x1 1.57 us: per_device(): field = spectrum.reshape(rows, points) * mask[None, :]]
    dot_general x5 -> x0, matrix products: 77 us -> none  [source_substep(): jnp.dot(kernel, block, precision=lax.Precision.HIGHEST, preferred_element...]
    pallas_call x0 -> x3, Pallas kernels: none -> 56.7 us  [the longest x1 36.8 us: per_device(): pl.pallas_call(functools.partial(source_kernel, freqs, blocks), out_shape...]
    reduce_sum x6 -> x0, other arithmetic: 37.9 us -> none  [the longest x5 36.4 us: source_substep(): steep = jnp.sum(wave_weight[None, :, None] * piece * piece, axis=(0, 1))]
    all_to_all x1 -> x2, waiting for transfers between devices: 6.5 us -> 43.7 us  [the longest x1 35.5 us: per_device(): mine = lax.all_to_all(moved, 'dir', split_axis=0, concat_axis=0, tiled=True)]
    all_to_all x0 -> x1, blocking collectives: none -> 25.9 us  [per_device(): lax.all_to_all(state.reshape(groups, rows, cols), 'dir', split_axis=0, co...]
  transfers between devices with their start and end apart: 8 -> 3, of which waited for: 8 -> 3; matrix products, arithmetic and copies ran while one was open for 1% -> 7% of each run, Pallas kernels for 0% -> 11%
where the time goes in v1:
time: 175 us; the launch traced here: 174 us
  Pallas kernels  56.7 us (32%)
  waiting for transfers between devices  51.4 us (29%)
  blocking collectives  25.9 us (15%)
  between operations  14.1 us (8%)
  local copies, waits for them, and re-layouts  12.5 us (7%)
  starting transfers between devices  10.7 us (6%)
  other arithmetic  2.42 us (1%)
    pallas_call x1, Pallas kernels, per_device(): pl.pallas_call(functools.partial(source_kernel, freqs, blocks), out_shape...  36.8 us
    all_to_all x1, waiting for transfers between devices, per_device(): mine = lax.all_to_all(moved, 'dir', split_axis=0, concat_axis=0, tiled=True)  35.5 us
    all_to_all x1, blocking collectives, per_device(): lax.all_to_all(state.reshape(groups, rows, cols), 'dir', split_axis=0, co...  25.9 us
    pallas_call x1, Pallas kernels, per_device(): pl.pallas_call(functools.partial(move_kernel, ways), grid=(groups,), out_...  15.9 us
    all_to_all x1, waiting for transfers between devices, per_device(): lax.all_to_all(outgoing, 'tile', split_axis=1, concat_axis=1, tiled=True)  8.24 us
    all_gather x1, waiting for transfers between devices, per_device(): full = lax.all_gather(kernel, 'dir', axis=0, tiled=True)  6.97 us
    all_to_all x1, starting transfers between devices, per_device(): lax.all_to_all(outgoing, 'tile', split_axis=1, concat_axis=1, tiled=True)  5.42 us
    all_to_all x1, starting transfers between devices, per_device(): mine = lax.all_to_all(moved, 'dir', split_axis=0, concat_axis=0, tiled=True)  5.3 us
  transfers between devices with their start and end apart: 3, of which 3 were waited for; matrix products, arithmetic and copies ran while one was open for 7% of the time, Pallas kernels for 11%

profile of v1, /device:TPU:1, one launch (start us, length us, event | category | flops | bytes accessed | tf_op | source)
XLA Modules:
  0.0 173.6 jit_solution(11585929820746198852)
XLA Ops:
  6.5 0.7 all-gather.2.cloned.1.call-update
  7.9 1.6 reshape.138
  9.5 1.4 broadcast_multiply_fusion.ext_ref.field_ref.block_ref
  10.9 4.0 %pick.1 = f32[216,512]{1,0:T(8,128)} custom-call(f32[216,2048]{1,0:T(8,128)} %broadcast_multiply_fusion.ext_ref.field_ref.block_ref, s32[1,512]{1,0:T(1,128)} %bitcast.38), custom_call_target="tpu_custom_call" | custom-call | tf_op jit(solution)/shard_map/pick/pallas_call | solution.py:129
  14.9 1.8 %copy_bitcast_fusion.1 = f32[216,4,128]{2,0,1:T(8,128)} fusion(f32[216,512]{1,0:T(8,128)} %pick.1), kind=kLoop, calls=%fused_computation.4 | loop fusion | bytes 884736 | tf_op jit(solution)/shard_map/all_to_all | solution.py:137
  16.7 5.4 %all-to-all-start = ((f32[216,4,128]{2,0,1:T(8,128)}), f32[216,4,128]{2,0,1:T(8,128)S(1)}, u32[]{:S(2)}, u32[]{:S(2)}) async-start(f32[216,4,128]{2,0,1:T(8,128)} %copy_bitcast_fusion.1), calls=%async_computation | async-start | bytes 884736 | tf_op jit(solution)/shard_map/all_to_all | solution.py:137
  22.1 0.1 fusion.1
  22.2 0.1 cosine_maximum_fusion
  22.3 0.6 gather_fusion.1
  22.9 0.1 compare_and_fusion
  23.0 0.1 select_bitcast_fusion
  23.1 0.1 broadcast_in_dim.34
  23.1 0.1 reshape.140
  23.2 0.8 copy.19.up_ref
  24.0 0.6 gather_fusion
  24.6 0.1 tile.7
  24.7 0.8 copy.20.speed_ref
  25.5 0.7 broadcast_select_fusion.idx_ref
  26.1 8.2 %all-to-all-done = f32[216,4,128]{2,0,1:T(8,128)S(1)} async-done(((f32[216,4,128]{2,0,1:T(8,128)}), f32[216,4,128]{2,0,1:T(8,128)S(1)}, u32[]{:S(2)}, u32[]{:S(2)}) %all-to-all-start) | async-done | bytes 442400 | tf_op jit(solution)/shard_map/all_to_all | solution.py:137
  34.4 0.8 copy_bitcast_fusion.halo_ref
  35.2 15.9 %move.1 = f32[8,216,256]{2,1,0:T(8,128)} custom-call(f32[216,2048]{1,0:T(8,128)} %broadcast_multiply_fusion.ext_ref.field_ref.block_ref, f32[216,512]{1,0:T(8,128)} %copy_bitcast_fusion.halo_ref, s32[2,2048]{1,0:T(2,128)} %broadcast_select_fusion.idx_ref, f32[216,2]{1,0:T(8,128)} %copy.19.up_ref, s32[1,2048]{1,0:T(1,128)} %bitcast.35, ...), custom_call_target="tpu_custom_call" | custom-call | tf_op jit(solution)/shard_map/move/pallas_call | solution.py:155
  51.1 5.3 %all-to-all-start.1 = ((f32[8,216,256]{2,1,0:T(8,128)}), f32[8,216,256]{2,1,0:T(8,128)S(1)}, u32[]{:S(2)}, u32[]{:S(2)}) async-start(f32[8,216,256]{2,1,0:T(8,128)} %move.1), calls=%async_computation.1 | async-start | bytes 3538944 | tf_op jit(solution)/shard_map/all_to_all | solution.py:174
  56.4 0.6 dynamic_slice.7
  57.0 1.3 dynamic_slice.6
  58.4 0.0 copy-done.3
  58.4 1.2 broadcast_in_dim_tile.4.weight_ref
  59.6 35.5 %all-to-all-done.1 = f32[8,216,256]{2,1,0:T(8,128)S(1)} async-done(((f32[8,216,256]{2,1,0:T(8,128)}), f32[8,216,256]{2,1,0:T(8,128)S(1)}, u32[]{:S(2)}, u32[]{:S(2)}) %all-to-all-start.1) | async-done | bytes 1769504 | tf_op jit(solution)/shard_map/all_to_all | solution.py:174
  95.1 7.0 %all-gather.2.cloned.1.call-done.kernel_ref = f32[1728,1728]{1,0:T(8,128)} async-done(((f32[216,1728]{1,0:T(8,128)}), f32[1728,1728]{1,0:T(8,128)}) %all-gather.2.cloned.1.call-update) | async-done | bytes 11943952 | tf_op jit(solution)/shard_map/all_gather | solution.py:124
  102.0 36.8 %source.1 = f32[1728,256]{1,0:T(8,128)} custom-call(f32[1728,256]{1,0:T(8,128)} %bitcast.32, f32[1,256]{1,0:T(1,128)} %bitcast.37, f32[1,256]{1,0:T(1,128)} %bitcast.36, f32[1728,1]{1,0:T(8,128)} %broadcast_in_dim_tile.4.weight_ref, f32[1728,1728]{1,0:T(8,128)} %all-gather.2.cloned.1.call-done.kernel_ref), custom_call_target="tpu_custom_call" | custom-call | tf_op jit(solution)/shard_map/source/pallas_call | solution.py:180
  138.8 25.9 %all_to_all.21 = f32[8,216,256]{2,1,0:T(8,128)S(1)} all-to-all(f32[8,216,256]{2,1,0:T(8,128)} %bitcast.33), channel_id=1, replica_groups=mesh['tile'=4,'dir'=8] {'dir'}, dimensions={0} | all-to-all | bytes 3538944 | tf_op jit(solution)/shard_map/all_to_all | solution.py:194
  164.7 0.6 copy.22
  165.2 1.6 reshape.143
  (14 shorter events, 0.0 us)
Async XLA Ops:
  6.5 17.5 %copy-start = (s32[4,2048]{1,0:T(4,128)S(1)}, s32[4,2048]{1,0:T(4,128)}, u32[]{:S(2)}) copy-start(s32[4,2048]{1,0:T(4,128)} %param.12) | copy-start | bytes 98308
  6.5 95.5 %all-gather.2.cloned.1.call-start = ((), (), s32[]{:S(2)}) async-start(), calls=%async_computation.3 | async-start | bytes 13934592 | tf_op jit(solution)/shard_map/all_gather | solution.py:124
  10.9 13.7 %copy-start.2 = (f32[4,36]{1,0:T(4,128)S(1)}, f32[4,36]{1,0:T(4,128)}, u32[]{:S(2)}) copy-start(f32[4,36]{1,0:T(4,128)} %param.14) | copy-start | bytes 1732
  16.7 17.7 %all-to-all-start = ((f32[216,4,128]{2,0,1:T(8,128)}), f32[216,4,128]{2,0,1:T(8,128)S(1)}, u32[]{:S(2)}, u32[]{:S(2)}) async-start(f32[216,4,128]{2,0,1:T(8,128)} %copy_bitcast_fusion.1), calls=%async_computation | async-start | bytes 884736 | tf_op jit(solution)/shard_map/all_to_all | solution.py:137
  51.1 7.2 %copy-start.3 = (f32[36]{0:T(128)S(1)}, f32[36]{0:T(128)}, u32[]{:S(2)}) copy-start(f32[36]{0:T(128)} %param.17) | copy-start | bytes 436
  51.1 43.9 %all-to-all-start.1 = ((f32[8,216,256]{2,1,0:T(8,128)}), f32[8,216,256]{2,1,0:T(8,128)S(1)}, u32[]{:S(2)}, u32[]{:S(2)}) async-start(f32[8,216,256]{2,1,0:T(8,128)} %move.1), calls=%async_computation.1 | async-start | bytes 3538944 | tf_op jit(solution)/shard_map/all_to_all | solution.py:174
  95.1 7.0 %copy-start.1 = (f32[8,216,256]{2,1,0:T(8,128)}, f32[8,216,256]{2,1,0:T(8,128)S(1)}, u32[]{:S(2)}) copy-start(f32[8,216,256]{2,1,0:T(8,128)S(1)} %all-to-all-done.1) | copy-start | bytes 5308420
Sparse Core Ops, SparseCore 0:
  9.3 92.7 all-gather.1

commit v2 on v1

--- a/solution.py
+++ b/solution.py
@@ -60,41 +60,111 @@
     out_ref[0] = own + courant * flow
 
 
-def source_kernel(freqs, blocks, moved_ref, turn_ref, mask_ref, weight_ref, kernel_ref, out_ref, khi_ref, klo_ref, shi_ref, slo_ref):
-    count, points = out_ref.shape
-    size = count // blocks
-
-    @pl.loop(0, blocks)
-    def _(i):
-        rows = pl.ds(pl.multiple_of(i * size, size), size)
-        hi, lo = split2(kernel_ref[rows, :])
-        khi_ref[rows, :] = hi
-        klo_ref[rows, :] = lo
+def source_kernel(
+    freqs, groups, moved_ref, turn_ref, mask_ref, weight_ref, half_ref, out_ref,
+    other_ref, khi_ref, klo_ref, state_ref, shi_ref, slo_ref, done_ref,
+    half_send, half_recv, send_sem, recv_sem,
+):
+    count, points = state_ref.shape
+    rows = count // groups
+    half = count // 2
+    size = half // 2
+    me = lax.axis_index("dir")
+    parity = lax.rem(me, 2)
+    twin = me + 1 - 2 * parity
+
+    barrier = pltpu.get_barrier_semaphore()
+    for r in range(1, groups):
+        pl.semaphore_signal(barrier, inc=1, device_id={"dir": lax.rem(me + r, groups)}, device_id_type=pl.DeviceIdType.MESH)
+    pl.semaphore_wait(barrier, groups - 1)
+
+    copies = []
+    for i in range(2):
+        copy = pltpu.make_async_remote_copy(
+            src_ref=half_ref.at[pl.ds(i * size, size)],
+            dst_ref=other_ref.at[pl.ds(i * size, size)],
+            send_sem=half_send.at[i],
+            recv_sem=half_recv.at[i],
+            device_id={"dir": twin},
+            device_id_type=pl.DeviceIdType.MESH,
+        )
+        copy.start()
+        copies.append(copy)
+
+    def split_rows(ref, i, base):
+        hi, lo = split2(ref[i * size:(i + 1) * size, :])
+        to = pl.ds(pl.multiple_of(base * half + i * size, 16), size)
+        khi_ref[to, :] = hi
+        klo_ref[to, :] = lo
 
     moved = moved_ref[...]
     forward = jnp.maximum(turn_ref[...], 0.0)
     backward = jnp.maximum(-turn_ref[...], 0.0)
     lower = pltpu.roll(moved, freqs, 0)
     upper = pltpu.roll(moved, count - freqs, 0)
-    out_ref[...] = moved + forward * (lower - moved) + backward * (upper - moved)
-    for step in range(SUB):
-        state = out_ref[...]
+    state_ref[...] = moved + forward * (lower - moved) + backward * (upper - moved)
+    for i in range(2):
+        split_rows(half_ref, i, parity)
+    for i in range(2):
+        copies[i].wait()
+        split_rows(other_ref, i, 1 - parity)
+
+    def send(target):
+        return pltpu.make_async_remote_copy(
+            src_ref=done_ref.at[target],
+            dst_ref=out_ref.at[:, pl.ds(pl.multiple_of(me * points, points), points)],
+            send_sem=send_sem.at[target],
+            recv_sem=recv_sem.at[me],
+            device_id={"dir": target},
+            device_id_type=pl.DeviceIdType.MESH,
+        )
+
+    def substep(last):
+        state = state_ref[...]
         steep = jnp.sum(weight_ref[...] * (state * state), axis=0, keepdims=True)
         scale = 1.0 / (1.0 + steep)
-        if step == SUB - 1:
+        if last:
             scale = scale * mask_ref[...]
         hi, lo = split2(state)
         shi_ref[...] = hi
         slo_ref[...] = lo
-
-        @pl.loop(0, blocks)
-        def _(i):
-            rows = pl.ds(pl.multiple_of(i * size, size), size)
-            khi = khi_ref[rows, :]
+        for h in range(2):
+            khi = khi_ref[h * half:(h + 1) * half, :]
             product = jnp.dot(khi, shi_ref[...], preferred_element_type=F32)
             product = product + jnp.dot(khi, slo_ref[...], preferred_element_type=F32)
-            product = product + jnp.dot(klo_ref[rows, :], shi_ref[...], preferred_element_type=F32)
-            out_ref[rows, :] = (out_ref[rows, :] + product) * scale
+            product = product + jnp.dot(klo_ref[h * half:(h + 1) * half, :], shi_ref[...], preferred_element_type=F32)
+            for j in range(groups // 2):
+                d = 2 * j + h
+                value = (state_ref[d * rows:(d + 1) * rows, :] + product[j * rows:(j + 1) * rows]) * scale
+                if last:
+                    done_ref[d] = value
+                else:
+                    state_ref[d * rows:(d + 1) * rows, :] = value
+            if last:
+                for j in range(groups // 2):
+                    target = 2 * lax.rem(me // 2 + 1 + j, groups // 2) + h
+
+                    @pl.when(target != me)
+                    def _():
+                        send(target).start()
+
+    @pl.loop(0, SUB - 1)
+    def _(step):
+        substep(False)
+
+    substep(True)
+    out_ref[:, pl.ds(pl.multiple_of(me * points, points), points)] = done_ref[me]
+    for r in range(1, groups):
+        other = lax.rem(me + r, groups)
+        send(other).wait_send()
+        pltpu.make_async_remote_copy(
+            src_ref=done_ref.at[other],
+            dst_ref=out_ref.at[:, pl.ds(pl.multiple_of(other * points, points), points)],
+            send_sem=send_sem.at[other],
+            recv_sem=recv_sem.at[other],
+            device_id={"dir": other},
+            device_id_type=pl.DeviceIdType.MESH,
+        ).wait_recv()
 
 
 def per_device(
@@ -121,7 +191,8 @@
     vmem = pltpu.CompilerParams(vmem_limit_bytes=56 * 2**20)
     whole = functools.partial(pl.BlockSpec, memory_space=pltpu.VMEM)
 
-    full = lax.all_gather(kernel, "dir", axis=0, tiled=True)
+    pairing = [list(range(c, groups, 2)) for c in range(2)]
+    half = lax.all_gather(kernel, "dir", axis=0, tiled=True, axis_index_groups=pairing)
 
     mask = (jnp.arange(points, dtype=jnp.int32) < active_points[0]).astype(F32)
     field = spectrum.reshape(rows, points) * mask[None, :]
@@ -176,23 +247,32 @@
     turn = lax.dynamic_slice_in_dim(refraction, start, cols)[None, :]
     my_mask = lax.dynamic_slice_in_dim(mask, start, cols)[None, :]
     weights = jnp.tile(wave_weight, total_dirs)[:, None]
-    blocks = 2
-    state = pl.pallas_call(
-        functools.partial(source_kernel, freqs, blocks),
-        out_shape=jax.ShapeDtypeStruct((count, cols), F32),
+    moved_cost = 2 * count * count * cols * 3 * SUB
+    result = pl.pallas_call(
+        functools.partial(source_kernel, freqs, groups),
+        out_shape=jax.ShapeDtypeStruct((rows, points), F32),
         in_specs=[whole()] * 5,
         out_specs=whole(),
         scratch_shapes=[
+            pltpu.VMEM((count // 2, count), F32),
             pltpu.VMEM((count, count), BF16),
             pltpu.VMEM((count, count), BF16),
+            pltpu.VMEM((count, cols), F32),
             pltpu.VMEM((count, cols), BF16),
             pltpu.VMEM((count, cols), BF16),
+            pltpu.VMEM((groups, rows, cols), F32),
+            pltpu.SemaphoreType.DMA((2,)),
+            pltpu.SemaphoreType.DMA((2,)),
+            pltpu.SemaphoreType.DMA((groups,)),
+            pltpu.SemaphoreType.DMA((groups,)),
         ],
-        compiler_params=vmem,
+        compiler_params=pltpu.CompilerParams(
+            vmem_limit_bytes=58 * 2**20, collective_id=0, has_side_effects=True
+        ),
+        cost_estimate=pl.CostEstimate(flops=moved_cost, bytes_accessed=4 * count * count, transcendentals=0),
         name="source",
-    )(mine.reshape(count, cols), turn, my_mask, weights, full)
-    back = lax.all_to_all(state.reshape(groups, rows, cols), "dir", split_axis=0, concat_axis=0, tiled=True)
-    return jnp.transpose(back, (1, 0, 2)).reshape(dirs_local, freqs, points)
+    )(mine.reshape(count, cols), turn, my_mask, weights, half)
+    return result.reshape(dirs_local, freqs, points)
 
 
 def solution(mesh):

time: 175 us -> 173 us (0.989)
  Pallas kernels: 56.7 us -> 82.9 us
  blocking collectives: 25.9 us -> 0 us
  waiting for transfers between devices: 51.4 us -> 48.9 us
    pallas_call x1, Pallas kernels: 36.8 us -> 63 us  [per_device(): pl.pallas_call(functools.partial(source_kernel, freqs, groups), out_shape...]
    all_to_all x1 -> x0, blocking collectives: 25.9 us -> none  [per_device(): lax.all_to_all(state.reshape(groups, rows, cols), 'dir', split_axis=0, co...]
    all_gather x1, waiting for transfers between devices: 6.97 us -> 4.54 us  [per_device(): lax.all_gather(kernel, 'dir', axis=0, tiled=True, axis_index_groups=pairing)]
  transfers between devices with their start and end apart: 3 -> 3, of which waited for: 3 -> 3; matrix products, arithmetic and copies ran while one was open for 7% -> 7% of each run, Pallas kernels for 11% -> 12%
where the time goes in v2:
time: 173 us; the launch traced here: 172 us
  Pallas kernels  82.9 us (48%)
  waiting for transfers between devices  48.9 us (28%)
  between operations  14.1 us (8%)
  local copies, waits for them, and re-layouts  13.1 us (8%)
  starting transfers between devices  10.7 us (6%)
  other arithmetic  2.43 us (1%)
    pallas_call x1, Pallas kernels, per_device(): pl.pallas_call(functools.partial(source_kernel, freqs, groups), out_shape...  63 us
    all_to_all x1, waiting for transfers between devices, per_device(): mine = lax.all_to_all(moved, 'dir', split_axis=0, concat_axis=0, tiled=True)  35.4 us
    pallas_call x1, Pallas kernels, per_device(): pl.pallas_call(functools.partial(move_kernel, ways), grid=(groups,), out_...  15.9 us
    all_to_all x1, waiting for transfers between devices, per_device(): lax.all_to_all(outgoing, 'tile', split_axis=1, concat_axis=1, tiled=True)  8.25 us
    all_to_all x1, starting transfers between devices, per_device(): lax.all_to_all(outgoing, 'tile', split_axis=1, concat_axis=1, tiled=True)  5.42 us
    all_to_all x1, starting transfers between devices, per_device(): mine = lax.all_to_all(moved, 'dir', split_axis=0, concat_axis=0, tiled=True)  5.3 us
    all_gather x1, waiting for transfers between devices, per_device(): lax.all_gather(kernel, 'dir', axis=0, tiled=True, axis_index_groups=pairing)  4.54 us
    pallas_call x1, Pallas kernels, per_device(): pl.pallas_call(pick_kernel, out_shape=jax.ShapeDtypeStruct((rows, tiles *...  3.95 us
  transfers between devices with their start and end apart: 3, of which 3 were waited for; matrix products, arithmetic and copies ran while one was open for 7% of the time, Pallas kernels for 12%

profile of v2, /device:TPU:1, one launch (start us, length us, event | category | flops | bytes accessed | tf_op | source)
XLA Modules:
  0.0 172.2 jit_solution(11939497117329728689)
XLA Ops:
  6.5 0.0 copy-start
  6.5 0.0 all-gather.2.cloned.1.call-start
  6.5 0.7 all-gather.2.cloned.1.call-update
  7.9 1.6 reshape.135
  9.5 1.4 broadcast_multiply_fusion.ext_ref.field_ref.block_ref
  10.9 4.0 %pick.1 = f32[216,512]{1,0:T(8,128)} custom-call(f32[216,2048]{1,0:T(8,128)} %broadcast_multiply_fusion.ext_ref.field_ref.block_ref, s32[1,512]{1,0:T(1,128)} %bitcast.32), custom_call_target="tpu_custom_call" | custom-call | tf_op jit(solution)/shard_map/pick/pallas_call | solution.py:200
  14.8 1.8 %copy_bitcast_fusion.1 = f32[216,4,128]{2,0,1:T(8,128)} fusion(f32[216,512]{1,0:T(8,128)} %pick.1), kind=kLoop, calls=%fused_computation.4 | loop fusion | bytes 884736 | tf_op jit(solution)/shard_map/all_to_all | solution.py:208
  16.7 5.4 %all-to-all-start = ((f32[216,4,128]{2,0,1:T(8,128)}), f32[216,4,128]{2,0,1:T(8,128)S(1)}, u32[]{:S(2)}, u32[]{:S(2)}) async-start(f32[216,4,128]{2,0,1:T(8,128)} %copy_bitcast_fusion.1), calls=%async_computation | async-start | bytes 884736 | tf_op jit(solution)/shard_map/all_to_all | solution.py:208
  22.1 0.1 fusion.1
  22.2 0.1 cosine_maximum_fusion
  22.3 0.6 gather_fusion.1
  22.8 0.1 compare_and_fusion
  22.9 0.1 select_bitcast_fusion
  23.0 0.1 broadcast_in_dim.34
  23.1 0.1 reshape.137
  23.2 0.8 copy.17.up_ref
  24.0 0.6 gather_fusion
  24.5 0.0 copy-done.2
  24.5 0.1 tile.7
  24.6 0.8 copy.18.speed_ref
  25.4 0.7 broadcast_select_fusion.idx_ref
  26.1 8.3 %all-to-all-done = f32[216,4,128]{2,0,1:T(8,128)S(1)} async-done(((f32[216,4,128]{2,0,1:T(8,128)}), f32[216,4,128]{2,0,1:T(8,128)S(1)}, u32[]{:S(2)}, u32[]{:S(2)}) %all-to-all-start) | async-done | bytes 442400 | tf_op jit(solution)/shard_map/all_to_all | solution.py:208
  34.3 0.9 copy_bitcast_fusion.halo_ref
  35.2 15.9 %move.1 = f32[8,216,256]{2,1,0:T(8,128)} custom-call(f32[216,2048]{1,0:T(8,128)} %broadcast_multiply_fusion.ext_ref.field_ref.block_ref, f32[216,512]{1,0:T(8,128)} %copy_bitcast_fusion.halo_ref, s32[2,2048]{1,0:T(2,128)} %broadcast_select_fusion.idx_ref, f32[216,2]{1,0:T(8,128)} %copy.17.up_ref, s32[1,2048]{1,0:T(1,128)} %bitcast.31, ...), custom_call_target="tpu_custom_call" | custom-call | tf_op jit(solution)/shard_map/move/pallas_call | solution.py:226
  51.1 5.3 %all-to-all-start.1 = ((f32[8,216,256]{2,1,0:T(8,128)}), f32[8,216,256]{2,1,0:T(8,128)S(1)}, u32[]{:S(2)}, u32[]{:S(2)}) async-start(f32[8,216,256]{2,1,0:T(8,128)} %move.1), calls=%async_computation.1 | async-start | bytes 3538944 | tf_op jit(solution)/shard_map/all_to_all | solution.py:245
  56.4 0.7 dynamic_slice.7
  57.1 1.3 dynamic_slice.6
  58.4 1.3 broadcast_in_dim_tile.4.weight_ref
  59.7 35.4 %all-to-all-done.1 = f32[8,216,256]{2,1,0:T(8,128)S(1)} async-done(((f32[8,216,256]{2,1,0:T(8,128)}), f32[8,216,256]{2,1,0:T(8,128)S(1)}, u32[]{:S(2)}, u32[]{:S(2)}) %all-to-all-start.1) | async-done | bytes 1769504 | tf_op jit(solution)/shard_map/all_to_all | solution.py:245
  95.1 4.5 %all-gather.2.cloned.1.call-done.half_ref = f32[864,1728]{1,0:T(8,128)} async-done(((f32[216,1728]{1,0:T(8,128)}), f32[864,1728]{1,0:T(8,128)}) %all-gather.2.cloned.1.call-update) | async-done | bytes 5971984 | tf_op jit(solution)/shard_map/all_gather | solution.py:195
  99.6 63.0 %source.1 = f32[216,2048]{1,0:T(8,128)} custom-call(f32[1728,256]{1,0:T(8,128)} %bitcast.30, f32[1,256]{1,0:T(1,128)} %bitcast.35, f32[1,256]{1,0:T(1,128)} %bitcast.34, f32[1728,1]{1,0:T(8,128)} %broadcast_in_dim_tile.4.weight_ref, f32[864,1728]{1,0:T(8,128)} %all-gather.2.cloned.1.call-done.half_ref), custom_call_target="tpu_custom_call" | custom-call | flops 22932357120 | bytes 11943936 | tf_op jit(solution)/shard_map/source/pallas_call | solution.py:251
  162.7 2.7 %reshape.139 = f32[6,36,2048]{2,1,0:T(8,128)} reshape(f32[216,2048]{1,0:T(8,128)} %source.1) | data formatting | bytes 3538944 | tf_op jit(solution)/shard_map/reshape | solution.py:275
  (12 shorter events, 0.0 us)
Async XLA Ops:
  6.5 17.4 %copy-start = (s32[4,2048]{1,0:T(4,128)S(1)}, s32[4,2048]{1,0:T(4,128)}, u32[]{:S(2)}) copy-start(s32[4,2048]{1,0:T(4,128)} %param.12) | copy-start | bytes 98308
  6.5 93.1 %all-gather.2.cloned.1.call-start = ((), (), s32[]{:S(2)}) async-start(), calls=%async_computation.2 | async-start | bytes 7741440 | tf_op jit(solution)/shard_map/all_gather | solution.py:195
  10.9 13.6 %copy-start.2 = (f32[4,36]{1,0:T(4,128)S(1)}, f32[4,36]{1,0:T(4,128)}, u32[]{:S(2)}) copy-start(f32[4,36]{1,0:T(4,128)} %param.14) | copy-start | bytes 1732
  16.7 17.7 %all-to-all-start = ((f32[216,4,128]{2,0,1:T(8,128)}), f32[216,4,128]{2,0,1:T(8,128)S(1)}, u32[]{:S(2)}, u32[]{:S(2)}) async-start(f32[216,4,128]{2,0,1:T(8,128)} %copy_bitcast_fusion.1), calls=%async_computation | async-start | bytes 884736 | tf_op jit(solution)/shard_map/all_to_all | solution.py:208
  51.1 7.3 %copy-start.3 = (f32[36]{0:T(128)S(1)}, f32[36]{0:T(128)}, u32[]{:S(2)}) copy-start(f32[36]{0:T(128)} %param.17) | copy-start | bytes 436
  51.1 43.9 %all-to-all-start.1 = ((f32[8,216,256]{2,1,0:T(8,128)}), f32[8,216,256]{2,1,0:T(8,128)S(1)}, u32[]{:S(2)}, u32[]{:S(2)}) async-start(f32[8,216,256]{2,1,0:T(8,128)} %move.1), calls=%async_computation.1 | async-start | bytes 3538944 | tf_op jit(solution)/shard_map/all_to_all | solution.py:245
  95.1 4.5 %copy-start.1 = (f32[8,216,256]{2,1,0:T(8,128)}, f32[8,216,256]{2,1,0:T(8,128)S(1)}, u32[]{:S(2)}) copy-start(f32[8,216,256]{2,1,0:T(8,128)S(1)} %all-to-all-done.1) | copy-start | bytes 5308420
Sparse Core Ops, SparseCore 0:
  9.2 90.3 all-gather.1

commit v3 on v2

--- a/solution.py
+++ b/solution.py
@@ -191,8 +191,14 @@
     vmem = pltpu.CompilerParams(vmem_limit_bytes=56 * 2**20)
     whole = functools.partial(pl.BlockSpec, memory_space=pltpu.VMEM)
 
-    pairing = [list(range(c, groups, 2)) for c in range(2)]
-    half = lax.all_gather(kernel, "dir", axis=0, tiled=True, axis_index_groups=pairing)
+    slots = groups // 2
+    twos = slots & (slots - 1) == 0
+    blocks = [(group // 2, kernel)]
+    for k in range(1, slots):
+        route = [(i, 2 * (((i // 2) ^ k) if twos else (i // 2 + k) % slots) + i % 2) for i in range(groups)]
+        came = lax.ppermute(kernel, "dir", route)
+        place = (group // 2) ^ k if twos else (group // 2 + slots - k) % slots
+        blocks.append((place, came))
 
     mask = (jnp.arange(points, dtype=jnp.int32) < active_points[0]).astype(F32)
     field = spectrum.reshape(rows, points) * mask[None, :]
@@ -247,6 +253,9 @@
     turn = lax.dynamic_slice_in_dim(refraction, start, cols)[None, :]
     my_mask = lax.dynamic_slice_in_dim(mask, start, cols)[None, :]
     weights = jnp.tile(wave_weight, total_dirs)[:, None]
+    half = jnp.zeros((count // 2, count), F32)
+    for place, block in blocks:
+        half = lax.dynamic_update_slice_in_dim(half, block, place * rows, 0)
     moved_cost = 2 * count * count * cols * 3 * SUB
     result = pl.pallas_call(
         functools.partial(source_kernel, freqs, groups),

time: 173 us -> 157 us (0.908)
  waiting for transfers between devices: 48.9 us -> 29.5 us
  between operations: 14.1 us -> 0.73 us
  local copies, waits for them, and re-layouts: 13.1 us -> 25 us
  Pallas kernels: 82.9 us -> 85.9 us
  starting transfers between devices: 10.7 us -> 13.4 us
    all_to_all x1, waiting for transfers between devices: 35.4 us -> 15.9 us  [per_device(): mine = lax.all_to_all(moved, 'dir', split_axis=0, concat_axis=0, tiled=True)]
    dynamic_update_slice x0 -> x4, local copies, waits for them, and re-layouts: none -> 7.79 us  [per_device(): half = lax.dynamic_update_slice_in_dim(half, block, place * rows, 0)]
    ppermute x0 -> x3, waiting for transfers between devices: none -> 5.43 us  [per_device(): came = lax.ppermute(kernel, 'dir', route)]
    all_gather x1 -> x0, waiting for transfers between devices: 4.54 us -> none  [per_device(): lax.all_gather(kernel, 'dir', axis=0, tiled=True, axis_index_groups=pairing)]
    ppermute x0 -> x3, starting transfers between devices: none -> 3.29 us  [per_device(): came = lax.ppermute(kernel, 'dir', route)]
    broadcast_in_dim x0 -> x1, local copies, waits for them, and re-layouts: none -> 3.02 us  [per_device(): half = jnp.zeros((count // 2, count), F32)]
    pallas_call x1, Pallas kernels: 63 us -> 66 us  [per_device(): pl.pallas_call(functools.partial(source_kernel, freqs, groups), out_shape...]
  transfers between devices with their start and end apart: 3 -> 5, of which waited for: 3 -> 3; matrix products, arithmetic and copies ran while one was open for 7% -> 15% of each run, Pallas kernels for 12% -> 13%
where the time goes in v3:
time: 157 us
  Pallas kernels  85.9 us (55%)
  waiting for transfers between devices  29.5 us (19%)
  local copies, waits for them, and re-layouts  25 us (16%)
  starting transfers between devices  13.4 us (9%)
  other arithmetic  2.43 us (2%)
    pallas_call x1, Pallas kernels, per_device(): pl.pallas_call(functools.partial(source_kernel, freqs, groups), out_shape...  66 us
    pallas_call x1, Pallas kernels, per_device(): pl.pallas_call(functools.partial(move_kernel, ways), grid=(groups,), out_...  16 us
    all_to_all x1, waiting for transfers between devices, per_device(): mine = lax.all_to_all(moved, 'dir', split_axis=0, concat_axis=0, tiled=True)  15.9 us
    all_to_all x1, waiting for transfers between devices, per_device(): lax.all_to_all(outgoing, 'tile', split_axis=1, concat_axis=1, tiled=True)  8.16 us
    dynamic_update_slice x4, local copies, waits for them, and re-layouts, per_device(): half = lax.dynamic_update_slice_in_dim(half, block, place * rows, 0)  7.79 us
    ppermute x3, waiting for transfers between devices, per_device(): came = lax.ppermute(kernel, 'dir', route)  5.43 us
    all_to_all x1, starting transfers between devices, per_device(): mine = lax.all_to_all(moved, 'dir', split_axis=0, concat_axis=0, tiled=True)  5.38 us
    all_to_all x1, starting transfers between devices, per_device(): lax.all_to_all(outgoing, 'tile', split_axis=1, concat_axis=1, tiled=True)  4.78 us
  transfers between devices with their start and end apart: 5, of which 3 were waited for; matrix products, arithmetic and copies ran while one was open for 15% of the time, Pallas kernels for 13%

profile of v3, /device:TPU:1, one launch (start us, length us, event | category | flops | bytes accessed | tf_op | source)
XLA Modules:
  0.0 157.0 jit_solution(6442878725728732728)
XLA Ops:
  0.0 2.0 %collective-permute-start = (f32[216,1728]{1,0:T(8,128)}, f32[216,1728]{1,0:T(8,128)}, u32[]{:S(2)}, u32[]{:S(2)}) collective-permute-start(f32[216,1728]{1,0:T(8,128)} %param.16), channel_id=1, source_target_pairs={{0,2},{1,3},{2,0},{3,1},{4,6},{5,7},{6,4},{7,5},{8,10},{9,11},{10,... | collective-permute-start | bytes 4478984 | tf_op jit(solution)/shard_map/ppermute | solution.py:199
  2.0 1.2 collective-permute-start.1
  4.0 1.6 reshape.135
  5.5 1.4 broadcast_multiply_fusion.ext_ref.field_ref.block_ref
  6.9 3.9 %pick.1 = f32[216,512]{1,0:T(8,128)} custom-call(f32[216,2048]{1,0:T(8,128)} %broadcast_multiply_fusion.ext_ref.field_ref.block_ref, s32[1,512]{1,0:T(1,128)} %bitcast.32), custom_call_target="tpu_custom_call" | custom-call | tf_op jit(solution)/shard_map/pick/pallas_call | solution.py:206
  10.9 1.8 %copy_bitcast_fusion.1 = f32[216,4,128]{2,0,1:T(8,128)} fusion(f32[216,512]{1,0:T(8,128)} %pick.1), kind=kLoop, calls=%fused_computation.4 | loop fusion | bytes 884736 | tf_op jit(solution)/shard_map/all_to_all | solution.py:214
  12.7 4.8 %all-to-all-start = ((f32[216,4,128]{2,0,1:T(8,128)}), f32[216,4,128]{2,0,1:T(8,128)S(1)}, u32[]{:S(2)}, u32[]{:S(2)}) async-start(f32[216,4,128]{2,0,1:T(8,128)} %copy_bitcast_fusion.1), calls=%async_computation | async-start | bytes 884736 | tf_op jit(solution)/shard_map/all_to_all | solution.py:214
  17.6 0.1 cosine_maximum_fusion
  17.7 0.6 gather_fusion.1
  18.2 0.1 compare_and_fusion
  18.5 0.1 reshape.137
  18.5 0.8 copy.17.up_ref
  19.3 0.6 gather_fusion
  20.0 0.8 copy.18.speed_ref
  20.8 0.7 broadcast_select_fusion.idx_ref
  21.5 8.2 %all-to-all-done = f32[216,4,128]{2,0,1:T(8,128)S(1)} async-done(((f32[216,4,128]{2,0,1:T(8,128)}), f32[216,4,128]{2,0,1:T(8,128)S(1)}, u32[]{:S(2)}, u32[]{:S(2)}) %all-to-all-start) | async-done | bytes 442400 | tf_op jit(solution)/shard_map/all_to_all | solution.py:214
  29.6 0.8 copy_bitcast_fusion.halo_ref
  30.4 16.0 %move.1 = f32[8,216,256]{2,1,0:T(8,128)} custom-call(f32[216,2048]{1,0:T(8,128)} %broadcast_multiply_fusion.ext_ref.field_ref.block_ref, f32[216,512]{1,0:T(8,128)} %copy_bitcast_fusion.halo_ref, s32[2,2048]{1,0:T(2,128)} %broadcast_select_fusion.idx_ref, f32[216,2]{1,0:T(8,128)} %copy.17.up_ref, s32[1,2048]{1,0:T(1,128)} %bitcast.31, ...), custom_call_target="tpu_custom_call" | custom-call | tf_op jit(solution)/shard_map/move/pallas_call | solution.py:232
  46.4 5.4 %all-to-all-start.1 = ((f32[8,216,256]{2,1,0:T(8,128)}), f32[8,216,256]{2,1,0:T(8,128)S(1)}, u32[]{:S(2)}, u32[]{:S(2)}) async-start(f32[8,216,256]{2,1,0:T(8,128)} %move.1), calls=%async_computation.1 | async-start | bytes 3538944 | tf_op jit(solution)/shard_map/all_to_all | solution.py:251
  51.8 0.7 dynamic_slice.7
  52.4 1.4 dynamic_slice.6
  53.8 1.2 broadcast_in_dim_tile.4.weight_ref
  55.0 3.0 %broadcast_in_dim.41 = f32[864,1728]{1,0:T(8,128)} broadcast(f32[]{:T(128)} %constant.82.clone.1), dimensions={} | broadcast | bytes 5971972 | tf_op jit(solution)/shard_map/broadcast_in_dim | solution.py:256
  58.0 1.2 constant_dynamic-update-slice_fusion.3
  59.2 2.6 %constant_dynamic-update-slice_fusion.2 = f32[864,1728]{1,0:T(8,128)} fusion(f32[864,1728]{1,0:T(8,128)} %constant_dynamic-update-slice_fusion.3, f32[216,1728]{1,0:T(8,128)} %collective-permute-done, s32[]{:T(128)S(6)} %select_n.68), kind=kLoop, calls=%fused_computation.16 | loop fusion | bytes 3096580 | tf_op jit(solution)/shard_map/dynamic_update_slice | solution.py:258
  61.9 2.6 %constant_dynamic-update-slice_fusion.1 = f32[864,1728]{1,0:T(8,128)} fusion(f32[864,1728]{1,0:T(8,128)} %constant_dynamic-update-slice_fusion.2, f32[216,1728]{1,0:T(8,128)} %collective-permute-done.1, s32[]{:T(128)S(6)} %select_n.69), kind=kLoop, calls=%fused_computation.15 | loop fusion | bytes 3096580 | tf_op jit(solution)/shard_map/dynamic_update_slice | solution.py:258
  64.5 5.4 %collective-permute-done.2 = f32[216,1728]{1,0:T(8,128)S(1)} collective-permute-done((f32[216,1728]{1,0:T(8,128)}, f32[216,1728]{1,0:T(8,128)S(1)}, u32[]{:S(2)}, u32[]{:S(2)}) %collective-permute-start.2) | collective-permute-done | bytes 1493024 | tf_op jit(solution)/shard_map/ppermute | solution.py:199
  70.0 1.3 constant_dynamic-update-slice_fusion.half_ref
  71.2 15.9 %all-to-all-done.1 = f32[8,216,256]{2,1,0:T(8,128)S(1)} async-done(((f32[8,216,256]{2,1,0:T(8,128)}), f32[8,216,256]{2,1,0:T(8,128)S(1)}, u32[]{:S(2)}, u32[]{:S(2)}) %all-to-all-start.1) | async-done | bytes 1769504 | tf_op jit(solution)/shard_map/all_to_all | solution.py:251
  87.1 1.2 copy-done.1
  88.3 66.0 %source.1 = f32[216,2048]{1,0:T(8,128)} custom-call(f32[1728,256]{1,0:T(8,128)} %bitcast.30, f32[1,256]{1,0:T(1,128)} %bitcast.35, f32[1,256]{1,0:T(1,128)} %bitcast.34, f32[1728,1]{1,0:T(8,128)} %broadcast_in_dim_tile.4.weight_ref, f32[864,1728]{1,0:T(8,128)} %constant_dynamic-update-slice_fusion.half_ref), custom_call_target="tpu_custom_call" | custom-call | flops 22932357120 | bytes 11943936 | tf_op jit(solution)/shard_map/source/pallas_call | solution.py:260
  154.3 2.7 %reshape.139 = f32[6,36,2048]{2,1,0:T(8,128)} reshape(f32[216,2048]{1,0:T(8,128)} %source.1) | data formatting | bytes 3538944 | tf_op jit(solution)/shard_map/reshape | solution.py:284
  (22 shorter events, 0.4 us)
Async XLA Ops:
  0.0 19.3 %copy-start = (s32[4,2048]{1,0:T(4,128)S(1)}, s32[4,2048]{1,0:T(4,128)}, u32[]{:S(2)}) copy-start(s32[4,2048]{1,0:T(4,128)} %param.12) | copy-start | bytes 98308
  0.0 59.2 %collective-permute-start = (f32[216,1728]{1,0:T(8,128)}, f32[216,1728]{1,0:T(8,128)}, u32[]{:S(2)}, u32[]{:S(2)}) collective-permute-start(f32[216,1728]{1,0:T(8,128)} %param.16), channel_id=1, source_target_pairs={{0,2},{1,3},{2,0},{3,1},{4,6},{5,7},{6,4},{7,5},{8,10},{9,11},{10,... | collective-permute-start | bytes 4478984 | tf_op jit(solution)/shard_map/ppermute | solution.py:199
  2.0 59.8 %collective-permute-start.1 = (f32[216,1728]{1,0:T(8,128)}, f32[216,1728]{1,0:T(8,128)}, u32[]{:S(2)}, u32[]{:S(2)}) collective-permute-start(f32[216,1728]{1,0:T(8,128)} %param.16), channel_id=1, source_target_pairs={{0,4},{1,5},{2,6},{3,7},{4,0},{5,1},{6,2},{7,3},{8,12},{9,13},{10,... | collective-permute-start | bytes 4478984 | tf_op jit(solution)/shard_map/ppermute | solution.py:199
  3.3 66.7 %collective-permute-start.2 = (f32[216,1728]{1,0:T(8,128)}, f32[216,1728]{1,0:T(8,128)S(1)}, u32[]{:S(2)}, u32[]{:S(2)}) collective-permute-start(f32[216,1728]{1,0:T(8,128)} %param.16), channel_id=1, source_target_pairs={{0,6},{1,7},{2,4},{3,5},{4,2},{5,3},{6,0},{7,1},{8,14},{9,15},{10,... | collective-permute-start | bytes 4478984 | tf_op jit(solution)/shard_map/ppermute | solution.py:199
  6.9 13.0 %copy-start.3 = (f32[4,36]{1,0:T(4,128)S(1)}, f32[4,36]{1,0:T(4,128)}, u32[]{:S(2)}) copy-start(f32[4,36]{1,0:T(4,128)} %param.14) | copy-start | bytes 1732
  12.7 16.9 %all-to-all-start = ((f32[216,4,128]{2,0,1:T(8,128)}), f32[216,4,128]{2,0,1:T(8,128)S(1)}, u32[]{:S(2)}, u32[]{:S(2)}) async-start(f32[216,4,128]{2,0,1:T(8,128)} %copy_bitcast_fusion.1), calls=%async_computation | async-start | bytes 884736 | tf_op jit(solution)/shard_map/all_to_all | solution.py:214
  46.4 7.4 %copy-start.4 = (f32[36]{0:T(128)S(1)}, f32[36]{0:T(128)}, u32[]{:S(2)}) copy-start(f32[36]{0:T(128)} %param.17) | copy-start | bytes 436
  46.4 40.7 %all-to-all-start.1 = ((f32[8,216,256]{2,1,0:T(8,128)}), f32[8,216,256]{2,1,0:T(8,128)S(1)}, u32[]{:S(2)}, u32[]{:S(2)}) async-start(f32[8,216,256]{2,1,0:T(8,128)} %move.1), calls=%async_computation.1 | async-start | bytes 3538944 | tf_op jit(solution)/shard_map/all_to_all | solution.py:251
  55.0 3.0 %copy-start.2 = (f32[216,1728]{1,0:T(8,128)S(1)}, f32[216,1728]{1,0:T(8,128)}, u32[]{:S(2)}) copy-start(f32[216,1728]{1,0:T(8,128)} %param.16) | copy-start | bytes 4478980
  87.1 1.2 copy-start.1

commit v4 on v3

--- a/solution.py
+++ b/solution.py
@@ -61,9 +61,9 @@
 
 
 def source_kernel(
-    freqs, groups, moved_ref, turn_ref, mask_ref, weight_ref, half_ref, out_ref,
-    other_ref, khi_ref, klo_ref, state_ref, shi_ref, slo_ref, done_ref,
-    half_send, half_recv, send_sem, recv_sem,
+    freqs, groups, moved_ref, turn_ref, mask_ref, weight_ref, half_ref, other_ref, out_ref,
+    khi_ref, klo_ref, state_ref, shi_ref, slo_ref, done_ref,
+    send_sem, recv_sem,
 ):
     count, points = state_ref.shape
     rows = count // groups
@@ -71,25 +71,11 @@
     size = half // 2
     me = lax.axis_index("dir")
     parity = lax.rem(me, 2)
-    twin = me + 1 - 2 * parity
 
     barrier = pltpu.get_barrier_semaphore()
     for r in range(1, groups):
         pl.semaphore_signal(barrier, inc=1, device_id={"dir": lax.rem(me + r, groups)}, device_id_type=pl.DeviceIdType.MESH)
     pl.semaphore_wait(barrier, groups - 1)
-
-    copies = []
-    for i in range(2):
-        copy = pltpu.make_async_remote_copy(
-            src_ref=half_ref.at[pl.ds(i * size, size)],
-            dst_ref=other_ref.at[pl.ds(i * size, size)],
-            send_sem=half_send.at[i],
-            recv_sem=half_recv.at[i],
-            device_id={"dir": twin},
-            device_id_type=pl.DeviceIdType.MESH,
-        )
-        copy.start()
-        copies.append(copy)
 
     def split_rows(ref, i, base):
         hi, lo = split2(ref[i * size:(i + 1) * size, :])
@@ -106,7 +92,6 @@
     for i in range(2):
         split_rows(half_ref, i, parity)
     for i in range(2):
-        copies[i].wait()
         split_rows(other_ref, i, 1 - parity)
 
     def send(target):
@@ -248,30 +233,28 @@
         name="move",
     )(field, incoming, links, up_rows, depth_class[None, :], speed_rows, field)
 
+    moved, half = lax.optimization_barrier((moved, jnp.zeros((count // 2, count), F32)))
     mine = lax.all_to_all(moved, "dir", split_axis=0, concat_axis=0, tiled=True)
     start = group * cols
     turn = lax.dynamic_slice_in_dim(refraction, start, cols)[None, :]
     my_mask = lax.dynamic_slice_in_dim(mask, start, cols)[None, :]
     weights = jnp.tile(wave_weight, total_dirs)[:, None]
-    half = jnp.zeros((count // 2, count), F32)
     for place, block in blocks:
         half = lax.dynamic_update_slice_in_dim(half, block, place * rows, 0)
+    other = lax.ppermute(half, "dir", [(i, i ^ 1) for i in range(groups)])
     moved_cost = 2 * count * count * cols * 3 * SUB
     result = pl.pallas_call(
         functools.partial(source_kernel, freqs, groups),
         out_shape=jax.ShapeDtypeStruct((rows, points), F32),
-        in_specs=[whole()] * 5,
+        in_specs=[whole()] * 6,
         out_specs=whole(),
         scratch_shapes=[
-            pltpu.VMEM((count // 2, count), F32),
             pltpu.VMEM((count, count), BF16),
             pltpu.VMEM((count, count), BF16),
             pltpu.VMEM((count, cols), F32),
             pltpu.VMEM((count, cols), BF16),
             pltpu.VMEM((count, cols), BF16),
             pltpu.VMEM((groups, rows, cols), F32),
-            pltpu.SemaphoreType.DMA((2,)),
-            pltpu.SemaphoreType.DMA((2,)),
             pltpu.SemaphoreType.DMA((groups,)),
             pltpu.SemaphoreType.DMA((groups,)),
         ],
@@ -280,7 +263,7 @@
         ),
         cost_estimate=pl.CostEstimate(flops=moved_cost, bytes_accessed=4 * count * count, transcendentals=0),
         name="source",
-    )(mine.reshape(count, cols), turn, my_mask, weights, half)
+    )(mine.reshape(count, cols), turn, my_mask, weights, half, other)
     return result.reshape(dirs_local, freqs, points)
 
 

time: 157 us -> 163 us (1.038)
  waiting for transfers between devices: 29.5 us -> 38.5 us
  Pallas kernels: 85.9 us -> 78.5 us
  starting transfers between devices: 13.4 us -> 16.2 us
    ppermute x3, waiting for transfers between devices: 5.43 us -> 14 us  [per_device(): came = lax.ppermute(kernel, 'dir', route)]
    pallas_call x1, Pallas kernels: 66 us -> 58.6 us  [per_device(): pl.pallas_call(functools.partial(source_kernel, freqs, groups), out_shape...]
    ppermute x0 -> x1, starting transfers between devices: none -> 4.43 us  [per_device(): other = lax.ppermute(half, 'dir', [(i, i ^ 1) for i in range(groups)])]
    all_to_all x1, starting transfers between devices: 5.38 us -> 3.72 us  [per_device(): mine = lax.all_to_all(moved, 'dir', split_axis=0, concat_axis=0, tiled=True)]
  transfers between devices with their start and end apart: 5 -> 6, of which waited for: 3 -> 3; matrix products, arithmetic and copies ran while one was open for 15% -> 14% of each run, Pallas kernels for 13% -> 12%
where the time goes in v4:
time: 163 us
  Pallas kernels  78.5 us (48%)
  waiting for transfers between devices  38.5 us (24%)
  local copies, waits for them, and re-layouts  26.5 us (16%)
  starting transfers between devices  16.2 us (10%)
  other arithmetic  2.45 us (2%)
    pallas_call x1, Pallas kernels, per_device(): pl.pallas_call(functools.partial(source_kernel, freqs, groups), out_shape...  58.6 us
    all_to_all x1, waiting for transfers between devices, per_device(): mine = lax.all_to_all(moved, 'dir', split_axis=0, concat_axis=0, tiled=True)  16.4 us
    pallas_call x1, Pallas kernels, per_device(): pl.pallas_call(functools.partial(move_kernel, ways), grid=(groups,), out_...  16 us
    ppermute x3, waiting for transfers between devices, per_device(): came = lax.ppermute(kernel, 'dir', route)  14 us
    dynamic_update_slice x4, local copies, waits for them, and re-layouts, per_device(): half = lax.dynamic_update_slice_in_dim(half, block, place * rows, 0)  9.25 us
    all_to_all x1, waiting for transfers between devices, per_device(): lax.all_to_all(outgoing, 'tile', split_axis=1, concat_axis=1, tiled=True)  8.15 us
    all_to_all x1, starting transfers between devices, per_device(): lax.all_to_all(outgoing, 'tile', split_axis=1, concat_axis=1, tiled=True)  4.77 us
    ppermute x1, starting transfers between devices, per_device(): other = lax.ppermute(half, 'dir', [(i, i ^ 1) for i in range(groups)])  4.43 us
  transfers between devices with their start and end apart: 6, of which 3 were waited for; matrix products, arithmetic and copies ran while one was open for 14% of the time, Pallas kernels for 12%

profile of v4, /device:TPU:1, one launch (start us, length us, event | category | flops | bytes accessed | tf_op | source)
XLA Modules:
  0.0 162.9 jit_solution(7020118113394672325)
XLA Ops:
  0.0 2.0 %collective-permute-start = (f32[216,1728]{1,0:T(8,128)}, f32[216,1728]{1,0:T(8,128)}, u32[]{:S(2)}, u32[]{:S(2)}) collective-permute-start(f32[216,1728]{1,0:T(8,128)} %param.16), channel_id=1, source_target_pairs={{0,2},{1,3},{2,0},{3,1},{4,6},{5,7},{6,4},{7,5},{8,10},{9,11},{10,... | collective-permute-start | bytes 4478984 | tf_op jit(solution)/shard_map/ppermute | solution.py:184
  2.0 1.2 collective-permute-start.1
  4.0 1.6 reshape.135
  5.5 1.4 broadcast_multiply_fusion.ext_ref.field_ref.block_ref
  6.9 4.0 %pick.1 = f32[216,512]{1,0:T(8,128)} custom-call(f32[216,2048]{1,0:T(8,128)} %broadcast_multiply_fusion.ext_ref.field_ref.block_ref, s32[1,512]{1,0:T(1,128)} %bitcast.32), custom_call_target="tpu_custom_call" | custom-call | tf_op jit(solution)/shard_map/pick/pallas_call | solution.py:191
  10.9 1.8 %copy_bitcast_fusion.1 = f32[216,4,128]{2,0,1:T(8,128)} fusion(f32[216,512]{1,0:T(8,128)} %pick.1), kind=kLoop, calls=%fused_computation.4 | loop fusion | bytes 884736 | tf_op jit(solution)/shard_map/all_to_all | solution.py:199
  12.7 4.8 %all-to-all-start = ((f32[216,4,128]{2,0,1:T(8,128)}), f32[216,4,128]{2,0,1:T(8,128)S(1)}, u32[]{:S(2)}, u32[]{:S(2)}) async-start(f32[216,4,128]{2,0,1:T(8,128)} %copy_bitcast_fusion.1), calls=%async_computation | async-start | bytes 884736 | tf_op jit(solution)/shard_map/all_to_all | solution.py:199
  17.6 0.1 cosine_maximum_fusion
  17.7 0.1 compare_and_fusion
  17.8 0.6 gather_fusion.1
  18.6 0.8 copy.17.up_ref
  19.4 0.6 gather_fusion
  20.0 0.8 copy.18.speed_ref
  20.8 0.7 broadcast_select_fusion.idx_ref
  21.5 8.2 %all-to-all-done = f32[216,4,128]{2,0,1:T(8,128)S(1)} async-done(((f32[216,4,128]{2,0,1:T(8,128)}), f32[216,4,128]{2,0,1:T(8,128)S(1)}, u32[]{:S(2)}, u32[]{:S(2)}) %all-to-all-start) | async-done | bytes 442400 | tf_op jit(solution)/shard_map/all_to_all | solution.py:199
  29.6 0.8 copy_bitcast_fusion.halo_ref
  30.5 16.0 %move.1 = f32[8,216,256]{2,1,0:T(8,128)} custom-call(f32[216,2048]{1,0:T(8,128)} %broadcast_multiply_fusion.ext_ref.field_ref.block_ref, f32[216,512]{1,0:T(8,128)} %copy_bitcast_fusion.halo_ref, s32[2,2048]{1,0:T(2,128)} %broadcast_select_fusion.idx_ref, f32[216,2]{1,0:T(8,128)} %copy.17.up_ref, s32[1,2048]{1,0:T(1,128)} %bitcast.31, ...), custom_call_target="tpu_custom_call" | custom-call | tf_op jit(solution)/shard_map/move/pallas_call | solution.py:217
  46.4 3.0 %broadcast_in_dim.39 = f32[864,1728]{1,0:T(8,128)} broadcast(f32[]{:T(128)} %constant.82.clone.1), dimensions={} | broadcast | bytes 5971972 | tf_op jit(solution)/shard_map/broadcast_in_dim | solution.py:236
  49.5 1.2 constant_dynamic-update-slice_fusion.3
  50.7 2.7 %constant_dynamic-update-slice_fusion.2 = f32[864,1728]{1,0:T(8,128)} fusion(f32[864,1728]{1,0:T(8,128)} %constant_dynamic-update-slice_fusion.3, f32[216,1728]{1,0:T(8,128)} %collective-permute-done, s32[]{:T(128)S(6)} %select_n.68), kind=kLoop, calls=%fused_computation.16 | loop fusion | bytes 3096580 | tf_op jit(solution)/shard_map/dynamic_update_slice | solution.py:243
  53.4 2.7 %constant_dynamic-update-slice_fusion.1 = f32[864,1728]{1,0:T(8,128)} fusion(f32[864,1728]{1,0:T(8,128)} %constant_dynamic-update-slice_fusion.2, f32[216,1728]{1,0:T(8,128)} %collective-permute-done.1, s32[]{:T(128)S(6)} %select_n.69), kind=kLoop, calls=%fused_computation.15 | loop fusion | bytes 3096580 | tf_op jit(solution)/shard_map/dynamic_update_slice | solution.py:243
  56.1 14.0 %collective-permute-done.2 = f32[216,1728]{1,0:T(8,128)} collective-permute-done((f32[216,1728]{1,0:T(8,128)}, f32[216,1728]{1,0:T(8,128)}, u32[]{:S(2)}, u32[]{:S(2)}) %collective-permute-start.2) | collective-permute-done | bytes 1493024 | tf_op jit(solution)/shard_map/ppermute | solution.py:184
  70.1 2.6 %constant_dynamic-update-slice_fusion.half_ref = f32[864,1728]{1,0:T(8,128)} fusion(f32[864,1728]{1,0:T(8,128)} %constant_dynamic-update-slice_fusion.1, f32[216,1728]{1,0:T(8,128)} %collective-permute-done.2, s32[]{:T(128)S(6)} %select_n.70), kind=kLoop, calls=%fused_computation.14 | loop fusion | bytes 3096580 | tf_op jit(solution)/shard_map/dynamic_update_slice | solution.py:243
  72.7 4.4 %collective-permute-start.3 = (f32[864,1728]{1,0:T(8,128)}, f32[864,1728]{1,0:T(8,128)}, u32[]{:S(2)}, u32[]{:S(2)}) collective-permute-start(f32[864,1728]{1,0:T(8,128)} %constant_dynamic-update-slice_fusion.half_ref), channel_id=1, source_target_pairs={{0,1},{1,0},{2,3},{3,2},{4,5},{5,4},{6,7},{7,6},{8,9},{9,8},{10,11... | collective-permute-start | bytes 17915912 | tf_op jit(solution)/shard_map/ppermute | solution.py:244
  77.1 3.7 %all-to-all-start.1 = ((f32[8,216,256]{2,1,0:T(8,128)}), f32[8,216,256]{2,1,0:T(8,128)S(1)}, u32[]{:S(2)}, u32[]{:S(2)}) async-start(f32[8,216,256]{2,1,0:T(8,128)} %move.1), calls=%async_computation.1 | async-start | bytes 3538944 | tf_op jit(solution)/shard_map/all_to_all | solution.py:237
  80.9 0.7 dynamic_slice.7
  81.5 1.3 dynamic_slice.6
  82.8 1.2 broadcast_in_dim_tile.4.weight_ref
  84.0 16.4 %all-to-all-done.1 = f32[8,216,256]{2,1,0:T(8,128)S(1)} async-done(((f32[8,216,256]{2,1,0:T(8,128)}), f32[8,216,256]{2,1,0:T(8,128)S(1)}, u32[]{:S(2)}, u32[]{:S(2)}) %all-to-all-start.1) | async-done | bytes 1769504 | tf_op jit(solution)/shard_map/all_to_all | solution.py:237
  100.4 1.2 copy-done.1
  101.6 58.6 %source.1 = f32[216,2048]{1,0:T(8,128)} custom-call(f32[1728,256]{1,0:T(8,128)} %bitcast.30, f32[1,256]{1,0:T(1,128)} %bitcast.35, f32[1,256]{1,0:T(1,128)} %bitcast.34, f32[1728,1]{1,0:T(8,128)} %broadcast_in_dim_tile.4.weight_ref, f32[864,1728]{1,0:T(8,128)} %constant_dynamic-update-slice_fusion.half_ref, f32[864,1728]{1,0:T(8,128)} %collective-permute-done.3.other_ref), custom_call_target="tpu_custom_call" | custom-call | flops 22932357120 | bytes 11943936 | tf_op jit(solution)/shard_map/source/pallas_call | solution.py:246
  160.3 2.7 %reshape.139 = f32[6,36,2048]{2,1,0:T(8,128)} reshape(f32[216,2048]{1,0:T(8,128)} %source.1) | data formatting | bytes 3538944 | tf_op jit(solution)/shard_map/reshape | solution.py:267
  (24 shorter events, 0.5 us)
Async XLA Ops:
  0.0 19.3 %copy-start = (s32[4,2048]{1,0:T(4,128)S(1)}, s32[4,2048]{1,0:T(4,128)}, u32[]{:S(2)}) copy-start(s32[4,2048]{1,0:T(4,128)} %param.12) | copy-start | bytes 98308
  0.0 50.7 %collective-permute-start = (f32[216,1728]{1,0:T(8,128)}, f32[216,1728]{1,0:T(8,128)}, u32[]{:S(2)}, u32[]{:S(2)}) collective-permute-start(f32[216,1728]{1,0:T(8,128)} %param.16), channel_id=1, source_target_pairs={{0,2},{1,3},{2,0},{3,1},{4,6},{5,7},{6,4},{7,5},{8,10},{9,11},{10,... | collective-permute-start | bytes 4478984 | tf_op jit(solution)/shard_map/ppermute | solution.py:184
  2.0 51.4 %collective-permute-start.1 = (f32[216,1728]{1,0:T(8,128)}, f32[216,1728]{1,0:T(8,128)}, u32[]{:S(2)}, u32[]{:S(2)}) collective-permute-start(f32[216,1728]{1,0:T(8,128)} %param.16), channel_id=1, source_target_pairs={{0,4},{1,5},{2,6},{3,7},{4,0},{5,1},{6,2},{7,3},{8,12},{9,13},{10,... | collective-permute-start | bytes 4478984 | tf_op jit(solution)/shard_map/ppermute | solution.py:184
  3.3 66.8 %collective-permute-start.2 = (f32[216,1728]{1,0:T(8,128)}, f32[216,1728]{1,0:T(8,128)}, u32[]{:S(2)}, u32[]{:S(2)}) collective-permute-start(f32[216,1728]{1,0:T(8,128)} %param.16), channel_id=1, source_target_pairs={{0,6},{1,7},{2,4},{3,5},{4,2},{5,3},{6,0},{7,1},{8,14},{9,15},{10,... | collective-permute-start | bytes 4478984 | tf_op jit(solution)/shard_map/ppermute | solution.py:184
  6.9 13.0 %copy-start.3 = (f32[4,36]{1,0:T(4,128)S(1)}, f32[4,36]{1,0:T(4,128)}, u32[]{:S(2)}) copy-start(f32[4,36]{1,0:T(4,128)} %param.14) | copy-start | bytes 1732
  12.7 16.9 %all-to-all-start = ((f32[216,4,128]{2,0,1:T(8,128)}), f32[216,4,128]{2,0,1:T(8,128)S(1)}, u32[]{:S(2)}, u32[]{:S(2)}) async-start(f32[216,4,128]{2,0,1:T(8,128)} %copy_bitcast_fusion.1), calls=%async_computation | async-start | bytes 884736 | tf_op jit(solution)/shard_map/all_to_all | solution.py:199
  46.4 3.0 %copy-start.2 = (f32[216,1728]{1,0:T(8,128)S(1)}, f32[216,1728]{1,0:T(8,128)}, u32[]{:S(2)}) copy-start(f32[216,1728]{1,0:T(8,128)} %param.16) | copy-start | bytes 4478980
  72.7 10.1 %copy-start.4 = (f32[36]{0:T(128)S(1)}, f32[36]{0:T(128)}, u32[]{:S(2)}) copy-start(f32[36]{0:T(128)} %param.17) | copy-start | bytes 436
  72.7 27.7 %collective-permute-start.3 = (f32[864,1728]{1,0:T(8,128)}, f32[864,1728]{1,0:T(8,128)}, u32[]{:S(2)}, u32[]{:S(2)}) collective-permute-start(f32[864,1728]{1,0:T(8,128)} %constant_dynamic-update-slice_fusion.half_ref), channel_id=1, source_target_pairs={{0,1},{1,0},{2,3},{3,2},{4,5},{5,4},{6,7},{7,6},{8,9},{9,8},{10,11... | collective-permute-start | bytes 17915912 | tf_op jit(solution)/shard_map/ppermute | solution.py:244
  77.1 23.3 %all-to-all-start.1 = ((f32[8,216,256]{2,1,0:T(8,128)}), f32[8,216,256]{2,1,0:T(8,128)S(1)}, u32[]{:S(2)}, u32[]{:S(2)}) async-start(f32[8,216,256]{2,1,0:T(8,128)} %move.1), calls=%async_computation.1 | async-start | bytes 3538944 | tf_op jit(solution)/shard_map/all_to_all | solution.py:237
  100.4 1.2 copy-start.1
